TPU v7x, 32 devices: a whole 2x2x4 slice. The times are simulated.
32 devices in a mesh: dp: 8 (over z, y), section: 4 (over x, core).
Axes of the slice: x: 2, y: 2, z: 4, core: 2. Of those that a mesh axis runs over, the one named last changes fastest.
Arguments:
- images: bfloat16 [32, 14, 14, 768], P(('dp', 'section')), may hold values from -6 to 6
- cotangent: bfloat16 [32, 14, 14, 768], P(('dp', 'section')), may hold values from -6 to 6
- window_rows: int32 [32], P('dp'), may hold values from 1 to 2
- window_cols: int32 [32], P('dp'), may hold values from 1 to 2
- pos_kernel: bfloat16 [4, 9, 768], P('section'), may hold values from -2 to 2
- pos_bias: bfloat16 [4, 768], P('section'), may hold values from -3 to 3
- norm_gain: bfloat16 [4, 768], P('section'), may hold values from 0.5 to 1.5
- norm_shift: bfloat16 [4, 768], P('section'), may hold values from -2 to 2
- first_weight: bfloat16 [4, 768, 3072], P('section'), may hold values from -1 to 1
- second_weight: bfloat16 [6144, 768], P('section'), may hold values from -0.15625 to 0.15625
Outputs:
- activations: bfloat16 [32, 14, 14, 768], P(('dp', 'section'))
- input_grad: float32 [32, 14, 14, 768], P(('dp', 'section'))
- first_grad: float32 [4, 768, 3072], P('section')
- second_grad: float32 [6144, 768], P('section')
- kernel_grad: float32 [4, 9, 768], P('section')
- bias_grad: float32 [4, 768], P('section')
- gain_grad: float32 [4, 768], P('section')
- shift_grad: float32 [4, 768], P('section')
Inputs may be any that keep to these rules, and one draw needn't show every extreme that they name: Image i covers the top 7 * window_rows[i] patch rows of its slot. Image i covers the left 7 * window_cols[i] patch columns of its slot.
All inputs are finite; a program needn't handle non-finite values.
Results may differ from a plain program's by a relative error of at most 0.035.
Values may be sent and summed in bfloat16 or wider, within the bound.
A program may use at most 576 MiB of HBM per device.

v0:
```python
from functools import partial

import jax
import jax.numpy as jnp
from jax import lax
from jax.experimental import pallas as pl
from jax.experimental.pallas import tpu as pltpu
from jax.sharding import PartitionSpec as P

D = 768
FF = 3072
HEADS = 24
HEAD = 32
WIN = 7
SIDE = 2
GRID = SIDE * WIN
CELL = 8
WROWS = WIN * CELL
HALF = GRID * CELL
ROWS = SIDE * HALF
GROUP = 256
PACK = GROUP // HEAD
NGROUP = D // GROUP
UNITS = NGROUP * SIDE * SIDE
LANE = 128
FTILE = 512
EPS = 1e-05
SCALE = HEAD ** (-0.5)
BF = jnp.bfloat16
F32 = jnp.float32
MESH = pl.DeviceIdType.MESH


def dot(a, b, ca=1, cb=0):
    return lax.dot_general(a, b, (((ca,), (cb,)), ((), ())), preferred_element_type=F32)


def lanes(index, width=LANE):
    return pl.ds(pl.multiple_of(index * width, width), width)


def halves(value):
    return value.reshape(SIDE, GRID, CELL, value.shape[-1])


def shifts(left, right):
    column = lax.broadcasted_iota(jnp.int32, left.shape, 1)
    before0 = pltpu.roll(left, 1, 1)
    after0 = jnp.where(column == WIN - 1, pltpu.roll(right, CELL - 2, 1), pltpu.roll(left, CELL - 1, 1))
    before1 = jnp.where(column == 0, pltpu.roll(left, 2, 1), pltpu.roll(right, 1, 1))
    after1 = pltpu.roll(right, CELL - 1, 1)
    return ((before0, left, after0), (before1, right, after1))


def gelu_parts(h):
    expo = jnp.exp(h * h * -0.5)
    t = 1.0 / (1.0 + (0.3275911 * 0.7071067811865476) * jnp.abs(h))
    poly = t * (0.127414796 + t * (-0.142248368 + t * (0.7107068705 + t * (-0.7265760135 + t * 0.5307027145))))
    tail = poly * expo
    phi = jnp.where(h >= 0, 1.0 - tail, tail)
    return h * phi, phi + h * expo * 0.3989422804014327


def front_forward(sec, m, ubuf, msk, pr, U, C, zz, xh, rs):
    zero = jnp.zeros((ROWS, LANE), F32)

    def conv(i, total):
        ls = lanes(i)
        u = ubuf[sec, m, :, ls].astype(F32)
        masked = halves(u * msk[m])
        U[0, 1 : GRID + 1, :, ls] = masked[0]
        U[1, 1 : GRID + 1, :, ls] = masked[1]
        moved = shifts(U[0, :, :, ls], U[1, :, :, ls])
        taps = pr[sec, :, ls]
        uh = halves(u)
        sums = []
        for wc in range(SIDE):
            acc = uh[wc] + taps[9:10, :][None]
            for a in range(3):
                for b in range(3):
                    acc = acc + moved[wc][b][a : a + GRID] * taps[3 * a + b : 3 * a + b + 1, :][None]
            acc = acc.reshape(HALF, LANE)
            C[pl.ds(wc * HALF, HALF), ls] = acc
            sums.append(acc)
        return total + jnp.concatenate(sums, axis=0)

    mean = jnp.sum(lax.fori_loop(0, D // LANE, conv, zero, unroll=True), axis=-1, keepdims=True) * (1.0 / D)

    def spread(i, total):
        centred = C[:, lanes(i)] - mean
        return total + centred * centred

    var = jnp.sum(lax.fori_loop(0, D // LANE, spread, zero, unroll=True), axis=-1, keepdims=True) * (1.0 / D)
    rstd = lax.rsqrt(var + EPS)
    rs[sec, m] = jnp.broadcast_to(rstd, (ROWS, LANE))

    def norm(i, carry):
        ls = lanes(i)
        xhat = (C[:, ls] - mean) * rstd
        xh[sec, m, :, ls] = xhat.astype(BF)
        zz[m, 2 * sec, :, ls] = (xhat * pr[sec, 10:11, ls] + pr[sec, 11:12, ls]).astype(BF)
        return carry

    lax.fori_loop(0, D // LANE, norm, 0, unroll=True)


def fold(value):
    return jnp.sum(value.reshape(ROWS // CELL, CELL, LANE), axis=0)


def front_backward(sec, m, msk, pr, U, T, gfull, xh, rs, sgp, out, sent):
    zero = jnp.zeros((ROWS, LANE), F32)

    def sums(i, carry):
        s1, s2 = carry
        ls = lanes(i)
        dz = T[:, ls]
        xhat = xh[sec, m, :, ls].astype(F32)
        both = xhat * dz
        sgp[sec, 10, :, ls] += fold(both)
        sgp[sec, 11, :, ls] += fold(dz)
        gain = pr[sec, 10:11, ls]
        return s1 + dz * gain, s2 + both * gain

    s1, s2 = lax.fori_loop(0, D // LANE, sums, (zero, zero), unroll=True)
    m1 = jnp.sum(s1, axis=-1, keepdims=True) * (1.0 / D)
    m2 = jnp.sum(s2, axis=-1, keepdims=True) * (1.0 / D)

    def back(i, carry):
        ls = lanes(i)
        xhat = xh[sec, m, :, ls].astype(F32)
        inner = T[:, ls] * pr[sec, 10:11, ls] - m1 - xhat * m2
        gc = gfull(i)[...].astype(F32) + rs[sec, m] * inner
        xh[sec, m, :, ls] = gc.astype(BF)
        gh = halves(gc)
        U[0, 1 : GRID + 1, :, ls] = gh[0]
        U[1, 1 : GRID + 1, :, ls] = gh[1]
        moved = shifts(U[0, :, :, ls], U[1, :, :, ls])
        taps = pr[sec, :, ls]
        mask = halves(msk[m])
        du = []
        for wc in range(SIDE):
            acc = jnp.zeros((GRID, CELL, LANE), F32)
            for a in range(3):
                for b in range(3):
                    tap = 3 * a + b
                    acc = acc + moved[wc][2 - b][2 - a : 2 - a + GRID] * taps[tap : tap + 1, :][None]
            du.append((gh[wc] + mask[wc] * acc).reshape(HALF, LANE))
        out(i)[...] = jnp.concatenate(du, axis=0).astype(BF)
        return carry

    lax.fori_loop(0, D // LANE // 2, back, 0, unroll=True)
    sent(0)
    lax.fori_loop(D // LANE // 2, D // LANE, back, 0, unroll=True)
    sent(1)


def front_sums(sec, m, ubuf, msk, U, xh, sgp):
    def part(i, carry):
        ls = lanes(i)
        gc = xh[sec, m, :, ls].astype(F32)
        sgp[sec, 9, :, ls] += fold(gc)
        gh = halves(gc)
        U[0, 1 : GRID + 1, :, ls] = gh[0]
        U[1, 1 : GRID + 1, :, ls] = gh[1]
        moved = shifts(U[0, :, :, ls], U[1, :, :, ls])
        um = halves(ubuf[sec, m, :, ls].astype(F32) * msk[m])
        for a in range(3):
            for b in range(3):
                kg = jnp.zeros((CELL, LANE), F32)
                for wc in range(SIDE):
                    kg = kg + jnp.sum(moved[wc][2 - b][2 - a : 2 - a + GRID] * um[wc], axis=0)
                sgp[sec, 3 * a + b, :, ls] += kg
        return carry

    lax.fori_loop(0, D // LANE, part, 0)


def spread_heads(value, head_of_lane):
    parts = [jnp.where(head_of_lane == h, value, 0.0) for h in range(PACK)]
    return jnp.concatenate(parts, axis=0).astype(BF)


def gather_heads(value, rows, head_of_lane):
    out = jnp.zeros((rows, GROUP), F32)
    for h in range(PACK):
        out = jnp.where(head_of_lane == h, value[h * rows : (h + 1) * rows], out)
    return out


def unit_slices(unit):
    pair, group = unit // NGROUP, lax.rem(unit, NGROUP)
    rows = [pl.ds(pl.multiple_of((2 * pair + w) * WROWS, 8), WROWS) for w in range(2)]
    cols = [pl.ds(pl.multiple_of(part * D + group * GROUP, LANE), GROUP) for part in range(3)]
    return rows, cols


def window_parts(m, i, qkv):
    rows, cols = unit_slices(i)
    head_of_lane = lax.broadcasted_iota(jnp.int32, (WROWS, GROUP), 1) // HEAD
    q = [qkv[m, r, cols[0]].astype(BF) for r in rows]
    kd = [spread_heads(qkv[m, r, cols[1]], head_of_lane) for r in rows]
    vd = [spread_heads(qkv[m, r, cols[2]], head_of_lane) for r in rows]
    return rows, cols, head_of_lane, q, kd, vd


def window_forward(m, qkv, pw, T, group):
    def unit(i):
        rows, cols, head_of_lane, q, kd, vd = window_parts(m, i, qkv)
        s = [(dot(b, a, 1, 1) * SCALE).reshape(PACK, WROWS, WROWS) for a, b in zip(q, kd)]
        key = lax.broadcasted_iota(jnp.int32, s[0].shape, 1)
        real = lax.rem(key, CELL) < WIN
        s = [jnp.where(real, x, -1e30) for x in s]
        p = [jnp.exp(x - jnp.max(x, axis=1, keepdims=True)) for x in s]
        p = [x * (1.0 / jnp.sum(x, axis=1, keepdims=True)) for x in p]
        p = [x.reshape(PACK * WROWS, WROWS) for x in p]
        for w in range(2):
            pw[m, 2 * i + w, :, 0:WROWS] = p[w]
        out = [dot(x.astype(BF), v, 0, 0) for x, v in zip(p, vd)]
        for w in range(2):
            T[rows[w], cols[0]] = out[w]

    for pair in range(UNITS // 2 // NGROUP):
        unit(pair * NGROUP + group)


def window_backward(m, qkv, pw, T):
    def unit(i, carry):
        rows, cols, head_of_lane, q, kd, vd = window_parts(m, i, qkv)
        g = [T[r, cols[0]].astype(BF) for r in rows]
        p = [pw[m, 2 * i + w, :, 0:WROWS].reshape(PACK, WROWS, WROWS) for w in range(2)]
        dp = [dot(v, x, 1, 1).reshape(PACK, WROWS, WROWS) for v, x in zip(vd, g)]
        ds = [x * (y - jnp.sum(x * y, axis=1, keepdims=True)) for x, y in zip(p, dp)]
        ds = [x.reshape(PACK * WROWS, WROWS).astype(BF) for x in ds]
        pb = [x.reshape(PACK * WROWS, WROWS).astype(BF) for x in p]
        dv = [gather_heads(dot(x, y), WROWS, head_of_lane) for x, y in zip(pb, g)]
        dk = [gather_heads(dot(x, y), WROWS, head_of_lane) * SCALE for x, y in zip(ds, q)]
        dq = [dot(x, y, 0, 0) * SCALE for x, y in zip(ds, kd)]
        for w in range(2):
            qkv[m, rows[w], cols[0]] = dq[w]
            qkv[m, rows[w], cols[1]] = dk[w]
            qkv[m, rows[w], cols[2]] = dv[w]
        return carry

    lax.fori_loop(0, UNITS // 2, unit, 0)


def group_slices(group):
    return [pl.ds(pl.multiple_of(part * D + group * GROUP, LANE), GROUP) for part in range(3)]


def channel_forward(m, qkv, pw, zz, msk):
    def unit(i, carry):
        cols = group_slices(i)
        mask = msk[m][:, :1]
        q = qkv[m, :, cols[0]].astype(BF)
        k = (qkv[m, :, cols[1]] * mask).astype(BF)
        v = qkv[m, :, cols[2]].astype(BF)
        s = dot(q, k, 0, 0) * SCALE
        same = (lax.broadcasted_iota(jnp.int32, s.shape, 0) // HEAD) == (lax.broadcasted_iota(jnp.int32, s.shape, 1) // HEAD)
        s = jnp.where(same, s, -1e30)
        p = jnp.exp(s - jnp.max(s, axis=1, keepdims=True))
        p = p * (1.0 / jnp.sum(p, axis=1, keepdims=True))
        for k in range(GROUP // LANE):
            pw[m, 2 * i + k, 0:GROUP, :] = p[:, k * LANE : (k + 1) * LANE]
        zz[m, 1, :, cols[0]] = dot(v, p.astype(BF), 1, 1).astype(BF)
        return carry

    lax.fori_loop(0, NGROUP, unit, 0, unroll=True)


def channel_backward(m, qkv, pw, T, rr, msk):
    def unit(i, carry):
        cols = group_slices(i)
        mask = msk[m][:, :1]
        q = qkv[m, :, cols[0]].astype(BF)
        k = (qkv[m, :, cols[1]] * mask).astype(BF)
        v = qkv[m, :, cols[2]].astype(BF)
        g = T[:, cols[0]].astype(BF)
        p = jnp.concatenate([pw[m, 2 * i + k, 0:GROUP, :] for k in range(GROUP // LANE)], axis=1)
        dp = dot(g, v, 0, 0)
        ds = (p * (dp - jnp.sum(p * dp, axis=1, keepdims=True))).astype(BF)
        rr[m, 0, :, cols[0]] = (dot(k, ds, 1, 1) * SCALE).astype(BF)
        rr[m, 0, :, cols[1]] = (dot(q, ds) * (SCALE * mask)).astype(BF)
        rr[m, 0, :, cols[2]] = (dot(g, p.astype(BF))).astype(BF)
        return carry

    lax.fori_loop(0, NGROUP, unit, 0, unroll=True)


RING = 8
COLS = FF // RING
WIDE = FF // 12 * 8 // RING
REST = FF // 3 // RING
THIRD = FF // 3 * 2
LENT = RING * 3 // 4
EARLY = 2


def relay_kernel(
    wrows, wcols, img, cot, kern, bias, gain, move, first, second,
    act, ing, out1, out2, outs,
    wf, w2, pr, msk, flat, ubuf, gin, gout, zz, xh, rs, qkv, ab, rr, pw, U, C, T, sgp, sgs, sgm,
    rL, rR, rA, rG, buf, acc, got,
    wl, ws, wr, pl_, usem, gsem, us, gs, ss, rsem, es, er, sgsem, ssem, rcem, osem, sms, smr, xs, xr, ys, yr, bs, br, hs, hr, free,
):
    n = RING
    s = lax.axis_index("section")
    dp = lax.axis_index("dp")
    stage, c = s // 2, lax.rem(s, 2)
    mate = (dp, stage * 2 + (1 - c))
    opposite = (dp, (1 - stage) * 2 + c)
    diagonal = (dp, 3 - s)
    lender, helper = s == 1, s == 2
    early = stage == 0

    spot = lax.rem(dp, n)
    base = dp - spot
    me = jnp.where(lax.rem(spot, 2) == 0, spot // 2, n - 1 - spot // 2)

    def place(pos):
        pos = lax.rem(pos + 2 * n, n)
        return (base + jnp.where(pos < n // 2, 2 * pos, 2 * (n - 1 - pos) + 1), s)

    nexts = (place(me + 1), place(me - 1))
    rounds = n.bit_length() - 1
    partners = []
    for r in range(rounds):
        bit = 1 << r
        partners.append((jnp.where(lax.rem(spot // bit, 2) == 0, dp + bit, dp - bit), s))

    barrier = pltpu.get_barrier_semaphore()
    peers = [mate, opposite, diagonal, *nexts, *partners]
    for peer in peers:
        pl.semaphore_signal(barrier, inc=1, device_id=peer, device_id_type=MESH)
    pl.semaphore_wait(barrier, len(peers))

    def remote(src, dst, send, recv, peer):
        return pltpu.make_async_remote_copy(
            src_ref=src, dst_ref=dst, send_sem=send, recv_sem=recv, device_id=peer, device_id_type=MESH
        )

    half = second.shape[0]

    def group_part(group, part):
        cols = pl.ds(pl.multiple_of(part * D + group * GROUP, LANE), GROUP)
        return first.at[:, cols], wf.at[0, :, cols]

    def wait_group(group):
        for part in range(3):
            src, dst = group_part(group, part)
            i = group * 3 + part

            @pl.when(c == 0)
            def _():
                pltpu.make_async_copy(src, dst, wl.at[i]).wait()

            @pl.when(c == 1)
            def _():
                remote(src, dst, ws.at[i], wr.at[i], mate).wait_recv()

    def weight_parts(k):
        parts = []
        if k == 0:
            for group in range(NGROUP):
                for part in range(3):
                    parts.append(group_part(group, part))
            cols = pl.ds(3 * D, D)
            parts.append((first.at[:, cols], wf.at[k, :, cols]))
        else:
            for i in range(3):
                cols = pl.ds(i * (FF // 3), FF // 3)
                parts.append((first.at[:, cols], wf.at[k, :, cols]))
        third = half // 3
        for i in range(3):
            rows = pl.ds(i * third, third)
            parts.append((second.at[rows, :], w2.at[pl.ds(k * half + i * third, third), :]))
        return parts

    names = (
        [f"qkv{group}" for group in range(NGROUP) for _ in range(3)] + ["out"] + [f"low{i}" for i in range(3)],
        ["in"] * 3 + [f"high{i}" for i in range(3)],
    )

    def weight_copies(k):
        local = [pltpu.make_async_copy(a, b, wl.at[i]) for i, (a, b) in enumerate(weight_parts(k))]
        sent = [remote(a, b, ws.at[i], wr.at[i], mate) for i, (a, b) in enumerate(weight_parts(k))]
        return local, sent

    def params_copy(k):
        return remote(pr.at[k], pr.at[k], ws.at[13], wr.at[13], mate)

    pr[c, 0:9, :] = kern[...].astype(F32)
    pr[c, 9:10, :] = bias[...].astype(F32)
    pr[c, 10:11, :] = gain[...].astype(F32)
    pr[c, 11:12, :] = move[...].astype(F32)
    params_copy(c).start()
    for k in range(2):

        @pl.when(c == k)
        def _():
            local, sent = weight_copies(k)
            for here, there in zip(local, sent):
                here.start()
                there.start()

    def wait_weights(*wanted):
        for k in range(2):

            @pl.when(c == k)
            def _():
                for name, copy in zip(names[k], weight_copies(k)[0]):
                    if name in wanted:
                        copy.wait()
                for name, copy in zip(names[1 - k], weight_copies(1 - k)[1]):
                    if name in wanted:
                        copy.wait_recv()

    def wait_params(k):
        @pl.when(c != k)
        def _():
            params_copy(k).wait_recv()

    raw = flat.at[0]
    img_out = remote(img, raw, pl_.at[0], pl_.at[1], opposite)
    cot_out = remote(cot, raw, pl_.at[0], pl_.at[1], opposite)

    def pad(src, dst):
        blank = jnp.zeros((CELL - WIN, D), F32)
        for r in range(GRID):
            line = src[r].astype(F32)
            for wc in range(SIDE):
                cells = jnp.concatenate([line[wc * WIN : (wc + 1) * WIN], blank], axis=0)
                C[pl.ds(wc * HALF + r * CELL, CELL), :] = cells
        dst[...] = C[...].astype(BF)

    def unpad(dst):
        for r in range(GRID):
            sides = [C[pl.ds(wc * HALF + r * CELL, CELL), :][:WIN] for wc in range(SIDE)]
            dst[r] = jnp.concatenate(sides, axis=0).astype(BF)

    @pl.when(early)
    def _():
        cot_out.start()
        pad(img, ubuf.at[0, 0])

    @pl.when(jnp.logical_not(early))
    def _():
        img_out.start()
        pad(cot, gin.at[1])

    index = lax.broadcasted_iota(jnp.int32, (ROWS, LANE), 0)
    cell = lax.rem(index, CELL)
    row = lax.rem(index, HALF) // CELL
    column = (index // HALF) * WIN + cell
    for m in range(2):
        inside = (row < WIN * wrows[c + 2 * m]) & (column < WIN * wcols[c + 2 * m]) & (cell < WIN)
        msk[m] = jnp.where(inside, 1.0, 0.0)

    @pl.when(jnp.logical_not(early))
    def _():
        cot_out.wait_recv()
        pad(raw, gin.at[0])
        for m in range(2):
            for l in range(D // LANE):
                cols = pl.ds(l * LANE, LANE)
                gin[m, :, cols] = (gin[m, :, cols].astype(F32) * msk[m]).astype(BF)

    for wc in range(SIDE):
        U[wc, 0] = jnp.zeros((CELL, D), F32)
        U[wc, GRID + 1] = jnp.zeros((CELL, D), F32)
    sgp[...] = jnp.zeros(sgp.shape, F32)

    def hop(m, dst, send, recv):
        sides = [pl.ds(i * D // 2, D // 2) for i in range(2)]
        return [
            remote(gout.at[m, :, cols], dst.at[:, cols], send.at[m, i], recv.at[m, i], opposite)
            for i, cols in enumerate(sides)
        ]

    def u_hop(m):
        return hop(m, ubuf.at[0, m], us, usem)

    def g_hop(m):
        return hop(m, gin.at[m], gs, gsem)

    def factor_copies(k, m):
        if k == 0:
            parts = [
                ("F0", zz.at[m, 0], rL.at[m, 0]),
                ("F1", zz.at[m, 1], rL.at[m, 1]),
                ("G", rr.at[m, 0, :, pl.ds(3 * D, D)], rR.at[m, :, pl.ds(3 * D, D)]),
                ("A", rr.at[m, 0, :, pl.ds(0, 3 * D)], rR.at[m, :, pl.ds(0, 3 * D)]),
            ]
        else:
            parts = [
                ("F2", zz.at[m, 2], rL.at[m, 0]),
                ("M", gin.at[m], rG.at[m]),
            ]
            parts.append(("X", ab.at[m], rA.at[m]))
            for i, cols in enumerate((pl.ds(0, FF // 3 * 2), pl.ds(FF // 3 * 2, FF // 3))):
                parts.append((f"H{i}", rr.at[m, 1, :, cols], rR.at[m, :, cols]))
        return [(w, remote(a, b, ss.at[m, i], rsem.at[m, i], mate)) for i, (w, a, b) in enumerate(parts)]

    def start_factors(m, which):
        for k in range(2):

            @pl.when(c != k)
            def _():
                for when, copy in factor_copies(k, m):
                    if when == which:
                        copy.start()

    def wait_factors(which):
        for k in range(2):

            @pl.when(c == k)
            def _():
                for m in range(2):
                    for when, copy in factor_copies(k, m):
                        if when[0] in which:
                            copy.wait_recv()

    def shard(k):
        return lax.rem(k + 4 * n, n)

    def sign(h):
        return 1 if h == 0 else -1

    def home(h, t):
        return shard(me + sign(h) - sign(h) * t)

    def products(terms):
        total = None
        for a, b in terms:
            part = dot(a[...], b[...], 0, 0)
            total = part if total is None else total + part
        return total

    def tile(sub, h, j):
        side = pl.ds(h * COLS, COLS)
        if sub in (0, 4):
            rows = first_rows(sub, h)
            last = jnp.where(j >= (3 * n) // 4, 1, 0)
            own = jnp.where(c == 1, 2, last)
            other = jnp.where(c == 1, 0, last)
            cols = lanes(j, COLS)
            terms = [(zz.at[m, own, :, rows], rr.at[m, c, :, cols]) for m in range(2)]
            terms += [(rL.at[m, other, :, rows], rR.at[m, :, cols]) for m in range(2)]
        elif sub == 3:
            cols = [pl.ds(pl.multiple_of(i * LENT * REST + j * REST, LANE), REST) for i in range(2)]
            terms = [(rA.at[m, :, cols[0]], rG.at[m, :, side]) for m in range(2)]
            terms += [(rA.at[m, :, cols[1]], gout.at[m, :, side]) for m in range(2)]
        else:
            cols = lanes(j, WIDE) if sub == 1 else pl.ds(pl.multiple_of(THIRD + j * REST, LANE), REST)
            terms = [(ab.at[m, :, cols], gin.at[m, :, side]) for m in range(2)]
            terms += [(rA.at[m, :, cols], rG.at[m, :, side]) for m in range(2)]
        return products(terms)

    sizes = (COLS // 3 * 2, WIDE, REST, REST, COLS // 3)
    starts = (0, COLS, COLS + WIDE, COLS + WIDE, COLS // 3 * 2)
    parts = [pl.ds(start, size) for start, size in zip(starts, sizes)]
    subs = range(len(sizes))
    odd = c == 1
    active = (None, odd, odd, helper, None)

    def where_live(sub, j, run):
        if sub == 2:
            pl.when(jnp.logical_not(lender) | (j >= LENT))(run)
        elif sub == 3:
            pl.when(j < LENT)(run)
        else:
            run()

    def first_rows(sub, h):
        return pl.ds(h * COLS + (0 if sub == 0 else sizes[0]), sizes[sub])

    def where_active(sub, run):
        if active[sub] is None:
            run()
        else:
            pl.when(active[sub])(run)


    def gathered(sub, h, j):
        if sub in (0, 4):
            return wf.at[0, first_rows(sub, h), lanes(j, COLS)]
        first_row = 0 if sub == 1 else THIRD
        return w2.at[pl.ds(pl.multiple_of(first_row + j * sizes[sub], 16), sizes[sub]), pl.ds(h * COLS, COLS)]

    def scatter(h, t, sub):
        src, dst = buf.at[h, t, parts[sub], :], buf.at[h, t + 1, parts[sub], :]
        return remote(src, dst, ssem.at[h, t, sub], rcem.at[h, t + 1, sub], nexts[h])

    def spread(h, t, sub, j):
        ref = gathered(sub, h, j)
        return remote(ref, ref, ssem.at[h, n - 1 + t, sub], rcem.at[h, n + t, sub], nexts[h])

    half_shards = n * 3 // 4

    def write(h, j, sub):
        src, side = gathered(sub, h, j), pl.ds(h * COLS, COLS)
        if sub in (0, 4):
            dst = out1.at[first_rows(sub, h), lanes(j, COLS)]
        elif sub == 1:
            dst = out2.at[pl.ds(pl.multiple_of((j - half_shards) * WIDE, 16), WIDE), side]
        else:
            dst = out2.at[pl.ds(pl.multiple_of(THIRD - FF // 2 + j * REST, 16), REST), side]
        if sub == 3:
            return remote(src, dst, bs.at[h, j], br.at[h, j], diagonal)
        return pltpu.make_async_copy(src, dst, osem.at[h, j, sub])

    def hand_over(h, j):
        dst = out2.at[pl.ds(pl.multiple_of(j * WIDE, 16), WIDE), pl.ds(h * COLS, COLS)]
        return remote(gathered(1, h, j), dst, hs.at[h, j], hr.at[h, j], mate)

    def deliver(h, j, sub):
        if sub == 1:

            @pl.when(j < half_shards)
            def _():
                hand_over(h, j).start()

            @pl.when(j >= half_shards)
            def _():
                write(h, j, sub).start()

        else:
            write(h, j, sub).start()

    def lend(m):
        cols, there = pl.ds(THIRD, LENT * REST), [rA.at[m, :, pl.ds(i * LENT * REST, LENT * REST)] for i in range(2)]
        return (
            remote(ab.at[m, :, cols], there[0], xs.at[m], xr.at[m], diagonal),
            remote(rA.at[m, :, cols], there[1], xs.at[2 + m], xr.at[2 + m], diagonal),
        )

    def share(m):
        return remote(gout.at[m], rG.at[m], ys.at[m], yr.at[m], mate)

    def reduce_event(sub, h, e):
        j = shard(me - sign(h) * e)

        @pl.when(e == n - 1)
        def _():
            pl.semaphore_wait(free.at[h, sub], 1)

        def run():
            total = tile(sub, h, j)

            @pl.when(e == 0)
            def _():
                buf[h, 0, parts[sub], :] = total.astype(BF)
                scatter(h, 0, sub).start()

            @pl.when((e > 0) & (e < n - 1))
            def _():
                scatter(h, e - 1, sub).wait_recv()
                buf[h, e, parts[sub], :] = (total + buf[h, e, parts[sub], :].astype(F32)).astype(BF)
                scatter(h, e, sub).start()

            @pl.when(e == n - 1)
            def _():
                scatter(h, n - 2, sub).wait_recv()
                gathered(sub, h, j)[...] = (total + buf[h, n - 1, parts[sub], :].astype(F32)).astype(BF)
                spread(h, 0, sub, j).start()
                deliver(h, j, sub)

        where_live(sub, j, run)

    def event(sub, e):
        for h in range(2):

            @pl.when(e < n)
            def _():
                reduce_event(sub, h, e)

            @pl.when((e >= n) & (e < 2 * n - 1))
            def _():
                t = e - (n - 1)
                j = home(h, t)

                def run():
                    spread(h, t - 1, sub, j).wait_recv()

                    @pl.when(t < n - 1)
                    def _():
                        spread(h, t, sub, j).start()

                    deliver(h, j, sub)

                where_live(sub, j, run)

    def early_event(e, which):
        @pl.when(odd)
        def _():
            for sub in which:
                where_active(sub, lambda: event(sub, e))

    def small(r):
        return remote(acc.at[r], got.at[r], sms.at[r], smr.at[r], partners[r])

    def mlp(m, order, wait):
        total, before, last = C[...], None, None
        for t in order:
            cols = pl.ds(t * FTILE, FTILE)
            h = dot(zz[m, 2], wf[1, :, cols])
            if last is not None:
                wait(last)
                total = total + dot(before, w2[pl.ds(last * FTILE, FTILE), :])
            a, d = gelu_parts(h)
            before, last = a.astype(BF), t
            ab[m, :, cols] = before
            rr[m, 1, :, cols] = d.astype(BF)
        wait(last)
        for i in range(2):
            cols = pl.ds(i * D // 2, D // 2)
            part = total[:, i * D // 2 : (i + 1) * D // 2]
            gout[m, :, cols] = (part + dot(before, w2[pl.ds(last * FTILE, FTILE), cols])).astype(BF)

            @pl.when(early)
            def _():
                u_hop(m)[i].start()

    def forward(m, p):
        @pl.when(jnp.logical_not(early))
        def _():
            for copy in u_hop(m):
                copy.wait_recv()

        @pl.when(early & (m == 1))
        def _():
            img_out.wait_recv()
            pad(raw, ubuf.at[0, 1])

        once = p == 0
        starting = early & once

        @pl.when(once)
        def _():
            wait_params(0)

        @pl.when(once & jnp.logical_not(early))
        def _():
            wait_params(1)
            wait_weights(*set(names[0] + names[1]))

        front_forward(0, m, ubuf, msk, pr, U, C, zz, xh, rs)
        start_factors(m, "F0")

        @pl.when(early)
        def _():
            def head_group(group, carry):
                @pl.when(once)
                def _():
                    wait_group(group)

                for part in range(3):
                    cols = pl.ds(pl.multiple_of(part * D + group * GROUP, LANE), GROUP)
                    qkv[m, :, cols] = dot(zz[m, 0], wf[0, :, cols])
                window_forward(m, qkv, pw, T, group)
                return carry

            lax.fori_loop(0, NGROUP, head_group, 0)
            zz[m, 1] = T[...].astype(BF)

        @pl.when(starting)
        def _():
            wait_weights("out")
            wait_params(1)

        @pl.when(jnp.logical_not(early))
        def _():
            for i in range(3):
                qkv[m, :, pl.ds(i * D, D)] = dot(zz[m, 0], wf[0, :, pl.ds(i * D, D)])

        @pl.when(jnp.logical_not(early))
        def _():
            channel_forward(m, qkv, pw, zz, msk)

        start_factors(m, "F1")
        ubuf[1, m] = (C[...] + dot(zz[m, 1], wf[0, :, pl.ds(3 * D, D)])).astype(BF)

        front_forward(1, m, ubuf, msk, pr, U, C, zz, xh, rs)
        start_factors(m, "F2")

        @pl.when(starting)
        def _():
            wait_weights("in")
            order = [i + 3 * k for i in range(3) for k in range(2)]
            mlp(m, order, lambda t: wait_weights(f"low{t}" if t < 3 else f"high{t - 3}"))

        @pl.when(jnp.logical_not(starting))
        def _():
            mlp(m, range(FF // FTILE), lambda t: None)

        start_factors(m, "X")

        @pl.when(jnp.logical_not(early))
        def _():
            for l in range(D // LANE):
                cols = pl.ds(l * LANE, LANE)
                C[:, cols] = gout[m, :, cols].astype(F32) * msk[m]
            unpad(flat.at[m])

        @pl.when(jnp.logical_not(early) & (m == 0))
        def _():
            remote(flat.at[0], act, es.at[0], er.at[0], opposite).start()

        @pl.when(jnp.logical_not(early) & (m == 1))
        def _():
            pltpu.make_async_copy(flat.at[1], act, es.at[0]).start()

        @pl.when(early & (m == 1))
        def _():
            wait_factors("FX")

        @pl.when(lender & (m == 1))
        def _():
            for i in range(2):
                for copy in lend(i):
                    copy.start()

    def backward(m):
        @pl.when(early)
        def _():
            for copy in g_hop(m):
                copy.wait_recv()

        start_factors(m, "M")
        for t in range(FF // FTILE):
            cols = pl.ds(t * FTILE, FTILE)
            da = dot(gin[m], w2[cols, :], 1, 1)
            rr[m, 1, :, cols] = (da * rr[m, 1, :, cols].astype(F32)).astype(BF)
            if t == FF // FTILE * 2 // 3 - 1:
                start_factors(m, "H0")

        start_factors(m, "H1")

        @pl.when(m == 1)
        def _():
            @pl.when(jnp.logical_not(early))
            def _():
                wait_factors("FX")

            wait_factors("M")
            early_event(0, (1, 2))

        T[...] = dot(rr[m, 1], wf[1], 1, 1)

        @pl.when(m == 1)
        def _():
            wait_factors("H")
            early_event(0, (0, 4))

        last = pl.ds(3 * D, D)

        @pl.when(early)
        def _():
            for copy in u_hop(m):
                copy.wait_send()

        def tail_lanes(i):
            return rr.at[m, 0, :, pl.ds(pl.multiple_of(3 * D + i * LANE, LANE), LANE)]

        def nothing(half):
            pass

        front_backward(1, m, msk, pr, U, T, lambda i: gin.at[m, :, lanes(i)], xh, rs, sgp, tail_lanes, nothing)
        start_factors(m, "G")

        T[...] = dot(rr[m, 0, :, last], wf[0, :, last], 1, 1)

        @pl.when(early)
        def _():
            window_backward(m, qkv, pw, T)
            for i in range(3):
                cols = pl.ds(i * D, D)
                rr[m, 0, :, cols] = qkv[m, :, cols].astype(BF)

        @pl.when(jnp.logical_not(early))
        def _():
            channel_backward(m, qkv, pw, T, rr, msk)

        start_factors(m, "A")

        @pl.when(m == 1)
        def _():
            for e in range(1, EARLY):
                early_event(e, (1, 2, 0, 4))

        T[...] = dot(rr[m, 0, :, pl.ds(0, 3 * D)], wf[0, :, pl.ds(0, 3 * D)], 1, 1)
        def send_half(half):
            @pl.when(jnp.logical_not(early))
            def _():
                g_hop(m)[half].start()

        front_backward(
            0, m, msk, pr, U, T, tail_lanes, xh, rs, sgp, lambda i: gout.at[m, :, lanes(i)], send_half
        )

        @pl.when(s == 3)
        def _():
            share(m).start()

        @pl.when(early)
        def _():
            C[...] = gout[m].astype(F32)
            unpad(flat.at[m])

        @pl.when(early & (m == 0))
        def _():
            pltpu.make_async_copy(flat.at[0], ing, es.at[1]).start()

        @pl.when(early & (m == 1))
        def _():
            remote(flat.at[1], ing, es.at[1], er.at[1], opposite).start()

    def phase(p, carry):
        m = jnp.where(early, lax.rem(p, 2), p // 2)
        ahead = jnp.where(early, p < 2, lax.rem(p, 2) == 0)

        @pl.when(ahead)
        def _():
            forward(m, p)

        @pl.when(jnp.logical_not(ahead))
        def _():
            backward(m)

        return carry

    lax.fori_loop(0, 4, phase, 0)

    for h in range(2):
        for sub in subs:

            def ready():
                pl.semaphore_signal(free.at[h, sub], inc=1, device_id=nexts[1 - h], device_id_type=MESH)

            where_active(sub, ready)

    give = remote(sgs.at[1 - c], sgm, sgsem.at[0], sgsem.at[1], mate)

    def small_sums():
        for sec in range(2):
            for j in range(12):
                sgs[sec, j : j + 1, :] = jnp.sum(sgp[sec, j], axis=0, keepdims=True)
            sgs[sec, 12:16, :] = jnp.zeros((4, D), F32)
        give.start()

    wait_factors("GA")

    @pl.when(helper)
    def _():
        for m in range(2):
            for copy in lend(m):
                copy.wait_recv()
            share(m).wait_recv()

    def ring_step(t, carry):
        for sub in (0, 4):
            event(sub, t + jnp.where(odd, EARLY, 0))
        where_active(1, lambda: event(1, t + EARLY))
        where_active(2, lambda: event(2, t + EARLY))
        where_active(3, lambda: event(3, t))
        @pl.when((t >= 1) & (t < 5))
        def _():
            front_sums((t - 1) // 2, lax.rem(t - 1, 2), ubuf, msk, U, xh, sgp)

        pl.when(t == 5)(small_sums)
        for r in range(rounds + 1):

            @pl.when(t == 6 + 2 * r)
            def _():
                if r == 0:
                    give.wait_recv()
                    acc[0] = sgs[c] + sgm[...]
                else:
                    small(r - 1).wait_recv()
                    acc[r] = acc[r - 1] + got[r - 1]
                if r < rounds:
                    small(r).start()

        return carry

    lax.fori_loop(0, 2 * n - 1, ring_step, 0)
    outs[...] = acc[rounds]

    for k in range(2):

        @pl.when(c == k)
        def _():
            for copy in weight_copies(k)[1]:
                copy.wait_send()
            params_copy(k).wait_send()
            for m in range(2):
                for _when, copy in factor_copies(1 - k, m):
                    copy.wait_send()

    give.wait_send()
    for r in range(rounds):
        small(r).wait_send()

    def drain(t, carry):
        for h in range(2):
            for sub in subs:

                def sent():
                    where_live(sub, shard(me - sign(h) * t), lambda: scatter(h, t, sub).wait_send())
                    where_live(sub, home(h, t), lambda: spread(h, t, sub, home(h, t)).wait_send())

                where_active(sub, sent)

        return carry

    lax.fori_loop(0, n - 1, drain, 0)

    def written(j, carry):
        for h in range(2):
            write(h, j, 0).wait()
            write(h, j, 4).wait()

            @pl.when(odd)
            def _():
                where_live(2, j, lambda: write(h, j, 2).wait())

                @pl.when(j < half_shards)
                def _():
                    hand_over(h, j).wait_send()

                @pl.when(j >= half_shards)
                def _():
                    write(h, j, 1).wait()

            @pl.when(jnp.logical_not(odd) & (j < half_shards))
            def _():
                hand_over(h, j).wait_recv()

            @pl.when(helper & (j < LENT))
            def _():
                write(h, j, 3).wait_send()

            @pl.when(lender & (j < LENT))
            def _():
                write(h, j, 3).wait_recv()

        return carry

    lax.fori_loop(0, n, written, 0)

    @pl.when(lender)
    def _():
        for m in range(2):
            for copy in lend(m):
                copy.wait_send()

    @pl.when(s == 3)
    def _():
        for m in range(2):
            share(m).wait_send()

    @pl.when(early)
    def _():
        cot_out.wait_send()
        pltpu.make_async_copy(flat.at[0], ing, es.at[1]).wait()
        remote(flat.at[1], ing, es.at[1], er.at[1], opposite).wait_send()
        remote(flat.at[0], act, es.at[0], er.at[0], opposite).wait_recv()

    @pl.when(jnp.logical_not(early))
    def _():
        img_out.wait_send()
        for m in range(2):
            for copy in g_hop(m):
                copy.wait_send()
        remote(flat.at[0], act, es.at[0], er.at[0], opposite).wait_send()
        pltpu.make_async_copy(flat.at[1], act, es.at[0]).wait()
        remote(flat.at[1], ing, es.at[1], er.at[1], opposite).wait_recv()


def relay(wrows, wcols, img, cot, kern, bias, gain, move, first, second):
    shape = jax.ShapeDtypeStruct
    vmem = pl.BlockSpec(memory_space=pltpu.VMEM)
    anywhere = pl.BlockSpec(memory_space=pl.ANY)
    dma = pltpu.SemaphoreType.DMA
    smem = pl.BlockSpec(memory_space=pltpu.SMEM)
    image = (ROWS, D)
    slot = img.shape
    rounds = RING.bit_length() - 1
    return pl.pallas_call(
        relay_kernel,
        out_shape=[
            shape(slot, BF),
            shape(slot, BF),
            shape((D, FF), BF),
            shape((FF // 2, D), BF),
            shape((16, D), F32),
        ],
        in_specs=[smem] * 2 + [vmem] * 6 + [anywhere] * 2,
        out_specs=[anywhere] * 4 + [vmem],
        scratch_shapes=[
            pltpu.VMEM((2, D, FF), BF),
            pltpu.VMEM((FF, D), BF),
            pltpu.VMEM((2, 16, D), F32),
            pltpu.VMEM((2, ROWS, LANE), F32),
            pltpu.VMEM((2,) + slot, BF),
            pltpu.VMEM((2, 2) + image, BF),
            pltpu.VMEM((2,) + image, BF),
            pltpu.VMEM((2,) + image, BF),
            pltpu.VMEM((2, 3) + image, BF),
            pltpu.VMEM((2, 2) + image, BF),
            pltpu.VMEM((2, 2, ROWS, LANE), F32),
            pltpu.VMEM((2, ROWS, 3 * D), F32),
            pltpu.VMEM((2, ROWS, FF), BF),
            pltpu.VMEM((2, 2, ROWS, FF), BF),
            pltpu.VMEM((2, UNITS, PACK * WROWS, LANE), F32),
            pltpu.VMEM((SIDE, GRID + 2, CELL, D), F32),
            pltpu.VMEM(image, F32),
            pltpu.VMEM(image, F32),
            pltpu.VMEM((2, 12, CELL, D), F32),
            pltpu.VMEM((2, 16, D), F32),
            pltpu.VMEM((16, D), F32),
            pltpu.VMEM((2, 2) + image, BF),
            pltpu.VMEM((2, ROWS, FF), BF),
            pltpu.VMEM((2, ROWS, FF), BF),
            pltpu.VMEM((2,) + image, BF),
            pltpu.VMEM((2, RING, COLS + WIDE + REST, COLS), BF),
            pltpu.VMEM((rounds + 1, 16, D), F32),
            pltpu.VMEM((rounds, 16, D), F32),
            dma((14,)),
            dma((14,)),
            dma((14,)),
            dma((2,)),
            dma((2, 2)),
            dma((2, 2)),
            dma((2, 2)),
            dma((2, 2)),
            dma((2, 8)),
            dma((2, 8)),
            dma((2,)),
            dma((2,)),
            dma((2,)),
            dma((2, 2 * RING, 5)),
            dma((2, 2 * RING, 5)),
            dma((2, RING, 5)),
            dma((rounds,)),
            dma((rounds,)),
            dma((4,)),
            dma((4,)),
            dma((2,)),
            dma((2,)),
            dma((2, RING)),
            dma((2, RING)),
            dma((2, RING)),
            dma((2, RING)),
            pltpu.SemaphoreType.REGULAR((2, 5)),
        ],
        name="relay",
        compiler_params=pltpu.CompilerParams(
            collective_id=1, has_side_effects=True, vmem_limit_bytes=63 * 2**20
        ),
    )(wrows, wcols, img, cot, kern, bias, gain, move, first, second)


def finish_kernel(
    out1, out2, act, ing, outs, first, second, acts, ings, kern, bias, gain, move,
    raw1, raw2, full1, full2, acted, graded, wide, small, kernels, rsem, wsem,
):
    steps = rsem.shape[0] - 3

    loads = [
        pltpu.make_async_copy(act, acted, rsem.at[steps]),
        pltpu.make_async_copy(ing, graded, rsem.at[steps + 1]),
        pltpu.make_async_copy(outs, small, rsem.at[steps + 2]),
    ]
    for copy in loads:
        copy.start()
    reads, writes = [], []
    for i in range(steps):
        pair = ((out1, raw1, full1, first), (out2, raw2, full2, second))[i % 2]
        src, raw, full, dst = pair
        half = steps // 2
        rows = pl.ds(i // 2 * (src.shape[0] // half), src.shape[0] // half)
        reads.append((pltpu.make_async_copy(src.at[rows, :], raw.at[rows, :], rsem.at[i]), raw, full, rows))
        writes.append(pltpu.make_async_copy(full.at[rows, :], dst.at[rows, :], wsem.at[i]))
    for copy, *_ in reads:
        copy.start()
    for (copy, raw, full, rows), back in zip(reads, writes):
        copy.wait()
        full[rows, :] = raw[rows, :].astype(F32)
        back.start()
    for copy in loads:
        copy.wait()
    for k in range(9):
        kernels[k] = small[k : k + 1, :]
    for r in range(GRID):
        line = graded[r].astype(F32)
        for k in range(GRID):
            wide[r, k] = line[k : k + 1, :]
    last = [
        pltpu.make_async_copy(acted, acts, wsem.at[steps]),
        pltpu.make_async_copy(wide, ings, wsem.at[steps + 1]),
        pltpu.make_async_copy(kernels, kern, wsem.at[steps + 2]),
    ]
    for i, dst in enumerate((bias, gain, move)):
        last.append(pltpu.make_async_copy(small.at[pl.ds(9 + i, 1), :], dst, wsem.at[steps + 3 + i]))
    for copy in last:
        copy.start()
    for copy in writes + last:
        copy.wait()


def finish(out1, out2, act, ing, outs):
    shape = jax.ShapeDtypeStruct
    slot = act.shape
    anywhere = pl.BlockSpec(memory_space=pl.ANY)
    line = (1, D)
    spread = slot[:2] + line
    steps = 16
    return pl.pallas_call(
        finish_kernel,
        out_shape=[
            shape(out1.shape, F32),
            shape(out2.shape, F32),
            shape(slot, BF),
            shape(spread, F32),
            shape((9,) + line, F32),
            shape(line, F32),
            shape(line, F32),
            shape(line, F32),
        ],
        in_specs=[anywhere] * 5,
        out_specs=[anywhere] * 8,
        scratch_shapes=[
            pltpu.VMEM(out1.shape, out1.dtype),
            pltpu.VMEM(out2.shape, out2.dtype),
            pltpu.VMEM(out1.shape, F32),
            pltpu.VMEM(out2.shape, F32),
            pltpu.VMEM(slot, BF),
            pltpu.VMEM(slot, BF),
            pltpu.VMEM(spread, F32),
            pltpu.VMEM(outs.shape, F32),
            pltpu.VMEM((9,) + line, F32),
            pltpu.SemaphoreType.DMA((steps + 3,)),
            pltpu.SemaphoreType.DMA((steps + 6,)),
        ],
        name="finish",
        compiler_params=pltpu.CompilerParams(vmem_limit_bytes=60 * 2**20),
    )(out1, out2, act, ing, outs)


def per_device(
    images, cotangent, window_rows, window_cols, pos_kernel, pos_bias, norm_gain, norm_shift, first_weight, second_weight
):
    act, ing, out1, out2, outs = relay(
        window_rows, window_cols, images[0], cotangent[0], pos_kernel[0], pos_bias, norm_gain, norm_shift,
        first_weight[0], second_weight,
    )
    if lax.axis_size("dp") > RING:
        out1, out2, outs = lax.psum((out1.astype(F32) / RING, out2.astype(F32) / RING, outs / RING), "dp")
    out1, out2, act, ing, kern, bias, gain, move = finish(out1, out2, act, ing, outs)
    return (
        act[None],
        ing.transpose(2, 0, 1, 3),
        out1[None],
        out2,
        kern.transpose(1, 0, 2),
        bias,
        gain,
        move,
    )


def solution(mesh):
    in_specs = (
        P(("dp", "section"), None, None, None),
        P(("dp", "section"), None, None, None),
        P("dp"),
        P("dp"),
        P("section", None, None),
        P("section", None),
        P("section", None),
        P("section", None),
        P("section", None, None),
        P("section", None),
    )
    out_specs = (
        P(("dp", "section"), None, None, None),
        P(("dp", "section"), None, None, None),
        P("section", None, None),
        P("section", None),
        P("section", None, None),
        P("section", None),
        P("section", None),
        P("section", None),
    )
    return jax.shard_map(per_device, mesh=mesh, in_specs=in_specs, out_specs=out_specs, check_vma=False)
```

profile of v0, /device:TPU:0, one launch (start us, length us, event | category | flops | bytes accessed | tf_op | source)
XLA Modules:
  0.0 222.8 jit_solution(7234311538210604663)
XLA Ops:
  0.6 214.4 %relay.1 = (bf16[14,14,768]{2,1,0:T(8,128)(2,1)}, bf16[14,14,768]{2,1,0:T(8,128)(2,1)}, bf16[768,3072]{1,0:T(8,128)(2,1)}, bf16[1536,768]{1,0:T(8,128)(2,1)}, f32[16,768]{1,0:T(8,128)}) custom-call(s32[4]{0:T(128)} %wrows.1, s32[4]{0:T(128)} %wcols.1, bf16[14,14,768]{2,1,0:T(8,128)(2,1)} %bitcast.9, bf16[14,14,768]{2,1,0:T(8,128)(2,1)} %bitcast.10, ...), custom_call_target="tpu_custom_call" | custom-call | tf_op jit(solution)/shard_map/relay/pallas_call | solution.py:1090
  215.1 7.6 %finish.1 = (f32[768,3072]{1,0:T(8,128)}, f32[1536,768]{1,0:T(8,128)}, bf16[14,14,768]{2,1,0:T(8,128)(2,1)}, f32[14,14,1,768]{3,2,1,0:T(1,128)}, f32[9,1,768]{2,...) custom-call(bf16[768,3072]{1,0:T(8,128)(2,1)} %get-tuple-element.21.out1, ...), custom_call_target="tpu_custom_call" | custom-call | tf_op jit(solution)/shard_map/finish/pallas_call | solution.py:1220
where the time goes:
time: 224 us; the launch traced here: 223 us
  Pallas kernels  222 us (99%)
    pallas_call x1, Pallas kernels, relay(): pl.pallas_call(relay_kernel, out_shape=[shape(slot, BF), shape(slot, BF),...  214 us
    pallas_call x1, Pallas kernels, finish(): pl.pallas_call(finish_kernel, out_shape=[shape(out1.shape, F32), shape(ou...  7.58 us

commit v1 on v0

--- a/solution.py
+++ b/solution.py
@@ -487,17 +487,17 @@
     def factor_copies(k, m):
         if k == 0:
             parts = [
-                ("F0", zz.at[m, 0], rL.at[m, 0]),
-                ("F1", zz.at[m, 1], rL.at[m, 1]),
-                ("G", rr.at[m, 0, :, pl.ds(3 * D, D)], rR.at[m, :, pl.ds(3 * D, D)]),
+                ("F", zz.at[m, 0], rL.at[m, 0]),
+                ("F", zz.at[m, 1], rL.at[m, 1]),
+                ("A", rr.at[m, 0, :, pl.ds(3 * D, D)], rR.at[m, :, pl.ds(3 * D, D)]),
                 ("A", rr.at[m, 0, :, pl.ds(0, 3 * D)], rR.at[m, :, pl.ds(0, 3 * D)]),
             ]
         else:
             parts = [
-                ("F2", zz.at[m, 2], rL.at[m, 0]),
+                ("F", zz.at[m, 2], rL.at[m, 0]),
                 ("M", gin.at[m], rG.at[m]),
             ]
-            parts.append(("X", ab.at[m], rA.at[m]))
+            parts.append(("F", ab.at[m], rA.at[m]))
             for i, cols in enumerate((pl.ds(0, FF // 3 * 2), pl.ds(FF // 3 * 2, FF // 3))):
                 parts.append((f"H{i}", rr.at[m, 1, :, cols], rR.at[m, :, cols]))
         return [(w, remote(a, b, ss.at[m, i], rsem.at[m, i], mate)) for i, (w, a, b) in enumerate(parts)]
@@ -716,11 +716,40 @@
         for i in range(2):
             cols = pl.ds(i * D // 2, D // 2)
             part = total[:, i * D // 2 : (i + 1) * D // 2]
-            gout[m, :, cols] = (part + dot(before, w2[pl.ds(last * FTILE, FTILE), cols])).astype(BF)
+            gout[jnp.where(early, m, 2 + m), :, cols] = (part + dot(before, w2[pl.ds(last * FTILE, FTILE), cols])).astype(BF)
 
             @pl.when(early)
             def _():
                 u_hop(m)[i].start()
+
+    def give_results(m):
+        @pl.when(early)
+        def _():
+            C[...] = gout[m].astype(F32)
+
+        @pl.when(jnp.logical_not(early))
+        def _():
+            for l in range(D // LANE):
+                cols = pl.ds(l * LANE, LANE)
+                C[:, cols] = gout[2 + m, :, cols].astype(F32) * msk[m]
+
+        unpad(flat.at[m])
+
+        @pl.when(early & (m == 0))
+        def _():
+            pltpu.make_async_copy(flat.at[0], ing, es.at[1]).start()
+
+        @pl.when(early & (m == 1))
+        def _():
+            remote(flat.at[1], ing, es.at[1], er.at[1], opposite).start()
+
+        @pl.when(jnp.logical_not(early) & (m == 0))
+        def _():
+            remote(flat.at[0], act, es.at[0], er.at[0], opposite).start()
+
+        @pl.when(jnp.logical_not(early) & (m == 1))
+        def _():
+            pltpu.make_async_copy(flat.at[1], act, es.at[0]).start()
 
     def forward(m, p):
         @pl.when(jnp.logical_not(early))
@@ -746,7 +775,6 @@
             wait_weights(*set(names[0] + names[1]))
 
         front_forward(0, m, ubuf, msk, pr, U, C, zz, xh, rs)
-        start_factors(m, "F0")
 
         @pl.when(early)
         def _():
@@ -778,11 +806,9 @@
         def _():
             channel_forward(m, qkv, pw, zz, msk)
 
-        start_factors(m, "F1")
         ubuf[1, m] = (C[...] + dot(zz[m, 1], wf[0, :, pl.ds(3 * D, D)])).astype(BF)
 
         front_forward(1, m, ubuf, msk, pr, U, C, zz, xh, rs)
-        start_factors(m, "F2")
 
         @pl.when(starting)
         def _():
@@ -794,26 +820,11 @@
         def _():
             mlp(m, range(FF // FTILE), lambda t: None)
 
-        start_factors(m, "X")
-
-        @pl.when(jnp.logical_not(early))
-        def _():
-            for l in range(D // LANE):
-                cols = pl.ds(l * LANE, LANE)
-                C[:, cols] = gout[m, :, cols].astype(F32) * msk[m]
-            unpad(flat.at[m])
-
-        @pl.when(jnp.logical_not(early) & (m == 0))
-        def _():
-            remote(flat.at[0], act, es.at[0], er.at[0], opposite).start()
-
-        @pl.when(jnp.logical_not(early) & (m == 1))
-        def _():
-            pltpu.make_async_copy(flat.at[1], act, es.at[0]).start()
+        start_factors(m, "F")
 
         @pl.when(early & (m == 1))
         def _():
-            wait_factors("FX")
+            wait_factors("F")
 
         @pl.when(lender & (m == 1))
         def _():
@@ -826,8 +837,8 @@
         def _():
             for copy in g_hop(m):
                 copy.wait_recv()
-
-        start_factors(m, "M")
+            start_factors(m, "M")
+
         for t in range(FF // FTILE):
             cols = pl.ds(t * FTILE, FTILE)
             da = dot(gin[m], w2[cols, :], 1, 1)
@@ -841,7 +852,7 @@
         def _():
             @pl.when(jnp.logical_not(early))
             def _():
-                wait_factors("FX")
+                wait_factors("F")
 
             wait_factors("M")
             early_event(0, (1, 2))
@@ -867,7 +878,6 @@
             pass
 
         front_backward(1, m, msk, pr, U, T, lambda i: gin.at[m, :, lanes(i)], xh, rs, sgp, tail_lanes, nothing)
-        start_factors(m, "G")
 
         T[...] = dot(rr[m, 0, :, last], wf[0, :, last], 1, 1)
 
@@ -903,18 +913,10 @@
         def _():
             share(m).start()
 
-        @pl.when(early)
-        def _():
-            C[...] = gout[m].astype(F32)
-            unpad(flat.at[m])
-
-        @pl.when(early & (m == 0))
-        def _():
-            pltpu.make_async_copy(flat.at[0], ing, es.at[1]).start()
-
-        @pl.when(early & (m == 1))
-        def _():
-            remote(flat.at[1], ing, es.at[1], er.at[1], opposite).start()
+    @pl.when(jnp.logical_not(early))
+    def _():
+        for m in range(2):
+            start_factors(m, "M")
 
     def phase(p, carry):
         m = jnp.where(early, lax.rem(p, 2), p // 2)
@@ -949,7 +951,7 @@
             sgs[sec, 12:16, :] = jnp.zeros((4, D), F32)
         give.start()
 
-    wait_factors("GA")
+    wait_factors("A")
 
     @pl.when(helper)
     def _():
@@ -969,6 +971,11 @@
             front_sums((t - 1) // 2, lax.rem(t - 1, 2), ubuf, msk, U, xh, sgp)
 
         pl.when(t == 5)(small_sums)
+
+        @pl.when((t >= 6) & (t < 8))
+        def _():
+            give_results(t - 6)
+
         for r in range(rounds + 1):
 
             @pl.when(t == 6 + 2 * r)
@@ -1106,7 +1113,7 @@
             pltpu.VMEM((2,) + slot, BF),
             pltpu.VMEM((2, 2) + image, BF),
             pltpu.VMEM((2,) + image, BF),
-            pltpu.VMEM((2,) + image, BF),
+            pltpu.VMEM((4,) + image, BF),
             pltpu.VMEM((2, 3) + image, BF),
             pltpu.VMEM((2, 2) + image, BF),
             pltpu.VMEM((2, 2, ROWS, LANE), F32),

time: 224 us -> 222 us (level)
  no operation moved by 1% of the time
where the time goes in v1:
time: 222 us; the launch traced here: 221 us
  Pallas kernels  220 us (99%)
    pallas_call x1, Pallas kernels, relay(): pl.pallas_call(relay_kernel, out_shape=[shape(slot, BF), shape(slot, BF),...  212 us
    pallas_call x1, Pallas kernels, finish(): pl.pallas_call(finish_kernel, out_shape=[shape(out1.shape, F32), shape(ou...  7.58 us

profile of v1, /device:TPU:0, one launch (start us, length us, event | category | flops | bytes accessed | tf_op | source)
XLA Modules:
  0.0 220.7 jit_solution(13167250797829423707)
XLA Ops:
  0.6 212.3 %relay.1 = (bf16[14,14,768]{2,1,0:T(8,128)(2,1)}, bf16[14,14,768]{2,1,0:T(8,128)(2,1)}, bf16[768,3072]{1,0:T(8,128)(2,1)}, bf16[1536,768]{1,0:T(8,128)(2,1)}, f32[16,768]{1,0:T(8,128)}) custom-call(s32[4]{0:T(128)} %wrows.1, s32[4]{0:T(128)} %wcols.1, bf16[14,14,768]{2,1,0:T(8,128)(2,1)} %bitcast.9, bf16[14,14,768]{2,1,0:T(8,128)(2,1)} %bitcast.10, ...), custom_call_target="tpu_custom_call" | custom-call | tf_op jit(solution)/shard_map/relay/pallas_call | solution.py:1097
  212.9 7.6 %finish.1 = (f32[768,3072]{1,0:T(8,128)}, f32[1536,768]{1,0:T(8,128)}, bf16[14,14,768]{2,1,0:T(8,128)(2,1)}, f32[14,14,1,768]{3,2,1,0:T(1,128)}, f32[9,1,768]{2,...) custom-call(bf16[768,3072]{1,0:T(8,128)(2,1)} %get-tuple-element.21.out1, ...), custom_call_target="tpu_custom_call" | custom-call | tf_op jit(solution)/shard_map/finish/pallas_call | solution.py:1227

commit v2 on v1

--- a/solution.py
+++ b/solution.py
@@ -301,7 +301,7 @@
     wrows, wcols, img, cot, kern, bias, gain, move, first, second,
     act, ing, out1, out2, outs,
     wf, w2, pr, msk, flat, ubuf, gin, gout, zz, xh, rs, qkv, ab, rr, pw, U, C, T, sgp, sgs, sgm,
-    rL, rR, rA, rG, buf, acc, got,
+    rL, rR, rA, rG, buf, acc, going, got,
     wl, ws, wr, pl_, usem, gsem, us, gs, ss, rsem, es, er, sgsem, ssem, rcem, osem, sms, smr, xs, xr, ys, yr, bs, br, hs, hr, free,
 ):
     n = RING
@@ -489,16 +489,16 @@
             parts = [
                 ("F", zz.at[m, 0], rL.at[m, 0]),
                 ("F", zz.at[m, 1], rL.at[m, 1]),
-                ("A", rr.at[m, 0, :, pl.ds(3 * D, D)], rR.at[m, :, pl.ds(3 * D, D)]),
+                ("G", rr.at[m, 0, :, pl.ds(3 * D, D)], rR.at[m, :, pl.ds(3 * D, D)]),
                 ("A", rr.at[m, 0, :, pl.ds(0, 3 * D)], rR.at[m, :, pl.ds(0, 3 * D)]),
             ]
         else:
             parts = [
-                ("F", zz.at[m, 2], rL.at[m, 0]),
+                ("X0", zz.at[m, 2], rL.at[m, 0]),
                 ("M", gin.at[m], rG.at[m]),
             ]
-            parts.append(("F", ab.at[m], rA.at[m]))
             for i, cols in enumerate((pl.ds(0, FF // 3 * 2), pl.ds(FF // 3 * 2, FF // 3))):
+                parts.append((f"X{i}", ab.at[m, :, cols], rA.at[m, :, cols]))
                 parts.append((f"H{i}", rr.at[m, 1, :, cols], rR.at[m, :, cols]))
         return [(w, remote(a, b, ss.at[m, i], rsem.at[m, i], mate)) for i, (w, a, b) in enumerate(parts)]
 
@@ -698,7 +698,7 @@
                 where_active(sub, lambda: event(sub, e))
 
     def small(r):
-        return remote(acc.at[r], got.at[r], sms.at[r], smr.at[r], partners[r])
+        return remote(going.at[r], got.at[r], sms.at[r], smr.at[r], partners[r])
 
     def mlp(m, order, wait):
         total, before, last = C[...], None, None
@@ -712,6 +712,8 @@
             before, last = a.astype(BF), t
             ab[m, :, cols] = before
             rr[m, 1, :, cols] = d.astype(BF)
+            if t == FF // FTILE * 2 // 3 - 1 and order == range(FF // FTILE):
+                start_factors(m, "X0")
         wait(last)
         for i in range(2):
             cols = pl.ds(i * D // 2, D // 2)
@@ -799,8 +801,7 @@
 
         @pl.when(jnp.logical_not(early))
         def _():
-            for i in range(3):
-                qkv[m, :, pl.ds(i * D, D)] = dot(zz[m, 0], wf[0, :, pl.ds(i * D, D)])
+            qkv[m] = dot(zz[m, 0], wf[0, :, pl.ds(0, 3 * D)])
 
         @pl.when(jnp.logical_not(early))
         def _():
@@ -815,16 +816,18 @@
             wait_weights("in")
             order = [i + 3 * k for i in range(3) for k in range(2)]
             mlp(m, order, lambda t: wait_weights(f"low{t}" if t < 3 else f"high{t - 3}"))
+            start_factors(m, "X0")
 
         @pl.when(jnp.logical_not(starting))
         def _():
             mlp(m, range(FF // FTILE), lambda t: None)
 
         start_factors(m, "F")
+        start_factors(m, "X1")
 
         @pl.when(early & (m == 1))
         def _():
-            wait_factors("F")
+            wait_factors("FX")
 
         @pl.when(lender & (m == 1))
         def _():
@@ -852,7 +855,7 @@
         def _():
             @pl.when(jnp.logical_not(early))
             def _():
-                wait_factors("F")
+                wait_factors("FX")
 
             wait_factors("M")
             early_event(0, (1, 2))
@@ -879,6 +882,7 @@
 
         front_backward(1, m, msk, pr, U, T, lambda i: gin.at[m, :, lanes(i)], xh, rs, sgp, tail_lanes, nothing)
 
+        start_factors(m, "G")
         T[...] = dot(rr[m, 0, :, last], wf[0, :, last], 1, 1)
 
         @pl.when(early)
@@ -951,7 +955,7 @@
             sgs[sec, 12:16, :] = jnp.zeros((4, D), F32)
         give.start()
 
-    wait_factors("A")
+    wait_factors("GA")
 
     @pl.when(helper)
     def _():
@@ -985,8 +989,9 @@
                     acc[0] = sgs[c] + sgm[...]
                 else:
                     small(r - 1).wait_recv()
-                    acc[r] = acc[r - 1] + got[r - 1]
+                    acc[r] = going[r - 1].astype(F32) + got[r - 1].astype(F32)
                 if r < rounds:
+                    going[r] = acc[r].astype(BF)
                     small(r).start()
 
         return carry
@@ -1133,7 +1138,8 @@
             pltpu.VMEM((2,) + image, BF),
             pltpu.VMEM((2, RING, COLS + WIDE + REST, COLS), BF),
             pltpu.VMEM((rounds + 1, 16, D), F32),
-            pltpu.VMEM((rounds, 16, D), F32),
+            pltpu.VMEM((rounds, 16, D), BF),
+            pltpu.VMEM((rounds, 16, D), BF),
             dma((14,)),
             dma((14,)),
             dma((14,)),

time: 222 us -> 222 us (level)
  no operation moved by 1% of the time
where the time goes in v2:
time: 222 us; the launch traced here: 221 us
  Pallas kernels  221 us (100%)
    pallas_call x1, Pallas kernels, relay(): pl.pallas_call(relay_kernel, out_shape=[shape(slot, BF), shape(slot, BF),...  213 us
    pallas_call x1, Pallas kernels, finish(): pl.pallas_call(finish_kernel, out_shape=[shape(out1.shape, F32), shape(ou...  7.58 us

profile of v2, /device:TPU:0, one launch (start us, length us, event | category | flops | bytes accessed | tf_op | source)
XLA Modules:
  0.0 221.4 jit_solution(17463166715264585603)
XLA Ops:
  0.6 213.0 %relay.1 = (bf16[14,14,768]{2,1,0:T(8,128)(2,1)}, bf16[14,14,768]{2,1,0:T(8,128)(2,1)}, bf16[768,3072]{1,0:T(8,128)(2,1)}, bf16[1536,768]{1,0:T(8,128)(2,1)}, f32[16,768]{1,0:T(8,128)}) custom-call(s32[4]{0:T(128)} %wrows.1, s32[4]{0:T(128)} %wcols.1, bf16[14,14,768]{2,1,0:T(8,128)(2,1)} %bitcast.9, bf16[14,14,768]{2,1,0:T(8,128)(2,1)} %bitcast.10, ...), custom_call_target="tpu_custom_call" | custom-call | tf_op jit(solution)/shard_map/relay/pallas_call | solution.py:1102
  213.6 7.6 %finish.1 = (f32[768,3072]{1,0:T(8,128)}, f32[1536,768]{1,0:T(8,128)}, bf16[14,14,768]{2,1,0:T(8,128)(2,1)}, f32[14,14,1,768]{3,2,1,0:T(1,128)}, f32[9,1,768]{2,...) custom-call(bf16[768,3072]{1,0:T(8,128)(2,1)} %get-tuple-element.21.out1, ...), custom_call_target="tpu_custom_call" | custom-call | tf_op jit(solution)/shard_map/finish/pallas_call | solution.py:1233

commit v3 on v2

--- a/solution.py
+++ b/solution.py
@@ -294,13 +294,12 @@
 REST = FF // 3 // RING
 THIRD = FF // 3 * 2
 LENT = RING * 3 // 4
-EARLY = 2
 
 
 def relay_kernel(
     wrows, wcols, img, cot, kern, bias, gain, move, first, second,
     act, ing, out1, out2, outs,
-    wf, w2, pr, msk, flat, ubuf, gin, gout, zz, xh, rs, qkv, ab, rr, pw, U, C, T, sgp, sgs, sgm,
+    kern_in, line_in, rows_in, cols_in, isem, wf, w2, pr, msk, flat, ubuf, gin, gout, zz, xh, rs, qkv, ab, rr, pw, U, C, T, sgp, sgs, sgm,
     rL, rR, rA, rG, buf, acc, going, got,
     wl, ws, wr, pl_, usem, gsem, us, gs, ss, rsem, es, er, sgsem, ssem, rcem, osem, sms, smr, xs, xr, ys, yr, bs, br, hs, hr, free,
 ):
@@ -390,11 +389,22 @@
     def params_copy(k):
         return remote(pr.at[k], pr.at[k], ws.at[13], wr.at[13], mate)
 
-    pr[c, 0:9, :] = kern[...].astype(F32)
-    pr[c, 9:10, :] = bias[...].astype(F32)
-    pr[c, 10:11, :] = gain[...].astype(F32)
-    pr[c, 11:12, :] = move[...].astype(F32)
-    params_copy(c).start()
+    own = flat.at[1]
+    small_inputs = [
+        pltpu.make_async_copy(a, b, isem.at[i])
+        for i, (a, b) in enumerate(
+            ((kern, kern_in), (bias, line_in.at[0]), (gain, line_in.at[1]), (move, line_in.at[2]), (wrows, rows_in), (wcols, cols_in))
+        )
+    ]
+    for copy in small_inputs:
+        copy.start()
+    img_in = pltpu.make_async_copy(img, own, isem.at[6])
+    cot_in = pltpu.make_async_copy(cot, own, isem.at[6])
+
+    @pl.when(early)
+    def _():
+        img_in.start()
+
     for k in range(2):
 
         @pl.when(c == k)
@@ -403,6 +413,13 @@
             for here, there in zip(local, sent):
                 here.start()
                 there.start()
+
+    for copy in small_inputs:
+        copy.wait()
+    pr[c, 0:9, :] = kern_in[...].astype(F32)
+    for i in range(3):
+        pr[c, 9 + i : 10 + i, :] = line_in[i].astype(F32)
+    params_copy(c).start()
 
     def wait_weights(*wanted):
         for k in range(2):
@@ -442,19 +459,22 @@
     @pl.when(early)
     def _():
         cot_out.start()
-        pad(img, ubuf.at[0, 0])
+        img_in.wait()
+        pad(own, ubuf.at[0, 0])
 
     @pl.when(jnp.logical_not(early))
     def _():
         img_out.start()
-        pad(cot, gin.at[1])
+        cot_in.start()
+        cot_in.wait()
+        pad(own, gin.at[1])
 
     index = lax.broadcasted_iota(jnp.int32, (ROWS, LANE), 0)
     cell = lax.rem(index, CELL)
     row = lax.rem(index, HALF) // CELL
     column = (index // HALF) * WIN + cell
     for m in range(2):
-        inside = (row < WIN * wrows[c + 2 * m]) & (column < WIN * wcols[c + 2 * m]) & (cell < WIN)
+        inside = (row < WIN * rows_in[c + 2 * m]) & (column < WIN * cols_in[c + 2 * m]) & (cell < WIN)
         msk[m] = jnp.where(inside, 1.0, 0.0)
 
     @pl.when(jnp.logical_not(early))
@@ -691,6 +711,8 @@
 
                 where_live(sub, j, run)
 
+    lead = jnp.where(early, 1, 2)
+
     def early_event(e, which):
         @pl.when(odd)
         def _():
@@ -858,7 +880,10 @@
                 wait_factors("FX")
 
             wait_factors("M")
-            early_event(0, (1, 2))
+
+            @pl.when(jnp.logical_not(early))
+            def _():
+                early_event(0, (1, 2))
 
         T[...] = dot(rr[m, 1], wf[1], 1, 1)
 
@@ -900,8 +925,8 @@
 
         @pl.when(m == 1)
         def _():
-            for e in range(1, EARLY):
-                early_event(e, (1, 2, 0, 4))
+            early_event(1, (0, 4))
+            early_event(lead - 1, (1, 2))
 
         T[...] = dot(rr[m, 0, :, pl.ds(0, 3 * D)], wf[0, :, pl.ds(0, 3 * D)], 1, 1)
         def send_half(half):
@@ -966,9 +991,9 @@
 
     def ring_step(t, carry):
         for sub in (0, 4):
-            event(sub, t + jnp.where(odd, EARLY, 0))
-        where_active(1, lambda: event(1, t + EARLY))
-        where_active(2, lambda: event(2, t + EARLY))
+            event(sub, t + jnp.where(odd, 2, 0))
+        where_active(1, lambda: event(1, t + lead))
+        where_active(2, lambda: event(2, t + lead))
         where_active(3, lambda: event(3, t))
         @pl.when((t >= 1) & (t < 5))
         def _():
@@ -1095,7 +1120,6 @@
     vmem = pl.BlockSpec(memory_space=pltpu.VMEM)
     anywhere = pl.BlockSpec(memory_space=pl.ANY)
     dma = pltpu.SemaphoreType.DMA
-    smem = pl.BlockSpec(memory_space=pltpu.SMEM)
     image = (ROWS, D)
     slot = img.shape
     rounds = RING.bit_length() - 1
@@ -1108,9 +1132,14 @@
             shape((FF // 2, D), BF),
             shape((16, D), F32),
         ],
-        in_specs=[smem] * 2 + [vmem] * 6 + [anywhere] * 2,
+        in_specs=[anywhere] * 10,
         out_specs=[anywhere] * 4 + [vmem],
         scratch_shapes=[
+            pltpu.VMEM(kern.shape, BF),
+            pltpu.VMEM((3,) + bias.shape, BF),
+            pltpu.SMEM(wrows.shape, jnp.int32),
+            pltpu.SMEM(wcols.shape, jnp.int32),
+            dma((7,)),
             pltpu.VMEM((2, D, FF), BF),
             pltpu.VMEM((FF, D), BF),
             pltpu.VMEM((2, 16, D), F32),

time: 222 us -> 225 us (1.014)
  Pallas kernels: 221 us -> 224 us
    pallas_call x1, Pallas kernels: 213 us -> 216 us  [relay(): pl.pallas_call(relay_kernel, out_shape=[shape(slot, BF), shape(slot, BF),...]
where the time goes in v3:
time: 225 us; the launch traced here: 224 us
  Pallas kernels  224 us (100%)
    pallas_call x1, Pallas kernels, relay(): pl.pallas_call(relay_kernel, out_shape=[shape(slot, BF), shape(slot, BF),...  216 us
    pallas_call x1, Pallas kernels, finish(): pl.pallas_call(finish_kernel, out_shape=[shape(out1.shape, F32), shape(ou...  7.58 us

profile of v3, /device:TPU:0, one launch (start us, length us, event | category | flops | bytes accessed | tf_op | source)
XLA Modules:
  0.0 224.3 jit_solution(15422988297772572377)
XLA Ops:
  0.6 216.0 %relay.1 = (bf16[14,14,768]{2,1,0:T(8,128)(2,1)}, bf16[14,14,768]{2,1,0:T(8,128)(2,1)}, bf16[768,3072]{1,0:T(8,128)(2,1)}, bf16[1536,768]{1,0:T(8,128)(2,1)}, f32[16,768]{1,0:T(8,128)}) custom-call(s32[4]{0:T(128)} %wrows.1, s32[4]{0:T(128)} %wcols.1, bf16[14,14,768]{2,1,0:T(8,128)(2,1)} %bitcast.9, bf16[14,14,768]{2,1,0:T(8,128)(2,1)} %bitcast.10, ...), custom_call_target="tpu_custom_call" | custom-call | tf_op jit(solution)/shard_map/relay/pallas_call | solution.py:1126
  216.6 7.6 %finish.1 = (f32[768,3072]{1,0:T(8,128)}, f32[1536,768]{1,0:T(8,128)}, bf16[14,14,768]{2,1,0:T(8,128)(2,1)}, f32[14,14,1,768]{3,2,1,0:T(1,128)}, f32[9,1,768]{2,...) custom-call(bf16[768,3072]{1,0:T(8,128)(2,1)} %get-tuple-element.21.out1, ...), custom_call_target="tpu_custom_call" | custom-call | tf_op jit(solution)/shard_map/finish/pallas_call | solution.py:1262

commit v4 on v3

--- a/solution.py
+++ b/solution.py
@@ -293,7 +293,8 @@
 WIDE = FF // 12 * 8 // RING
 REST = FF // 3 // RING
 THIRD = FF // 3 * 2
-LENT = RING * 3 // 4
+LENT = RING * 7 // 8
+EARLY = 2
 
 
 def relay_kernel(
@@ -711,8 +712,6 @@
 
                 where_live(sub, j, run)
 
-    lead = jnp.where(early, 1, 2)
-
     def early_event(e, which):
         @pl.when(odd)
         def _():
@@ -880,10 +879,7 @@
                 wait_factors("FX")
 
             wait_factors("M")
-
-            @pl.when(jnp.logical_not(early))
-            def _():
-                early_event(0, (1, 2))
+            early_event(0, (1, 2))
 
         T[...] = dot(rr[m, 1], wf[1], 1, 1)
 
@@ -925,8 +921,7 @@
 
         @pl.when(m == 1)
         def _():
-            early_event(1, (0, 4))
-            early_event(lead - 1, (1, 2))
+            early_event(1, (1, 2, 0, 4))
 
         T[...] = dot(rr[m, 0, :, pl.ds(0, 3 * D)], wf[0, :, pl.ds(0, 3 * D)], 1, 1)
         def send_half(half):
@@ -991,9 +986,9 @@
 
     def ring_step(t, carry):
         for sub in (0, 4):
-            event(sub, t + jnp.where(odd, 2, 0))
-        where_active(1, lambda: event(1, t + lead))
-        where_active(2, lambda: event(2, t + lead))
+            event(sub, t + jnp.where(odd, EARLY, 0))
+        where_active(1, lambda: event(1, t + EARLY))
+        where_active(2, lambda: event(2, t + EARLY))
         where_active(3, lambda: event(3, t))
         @pl.when((t >= 1) & (t < 5))
         def _():

time: 225 us -> 222 us (0.987); the launches traced: 224 us -> 219 us
  Pallas kernels: 224 us -> 218 us
    pallas_call x1, Pallas kernels: 216 us -> 211 us  [relay(): pl.pallas_call(relay_kernel, out_shape=[shape(slot, BF), shape(slot, BF),...]
where the time goes in v4:
time: 222 us; the launch traced here: 219 us
  Pallas kernels  218 us (98%)
    pallas_call x1, Pallas kernels, relay(): pl.pallas_call(relay_kernel, out_shape=[shape(slot, BF), shape(slot, BF),...  211 us
    pallas_call x1, Pallas kernels, finish(): pl.pallas_call(finish_kernel, out_shape=[shape(out1.shape, F32), shape(ou...  7.58 us

profile of v4, /device:TPU:0, one launch (start us, length us, event | category | flops | bytes accessed | tf_op | source)
XLA Modules:
  0.0 219.0 jit_solution(7045243801138268685)
XLA Ops:
  0.6 210.7 %relay.1 = (bf16[14,14,768]{2,1,0:T(8,128)(2,1)}, bf16[14,14,768]{2,1,0:T(8,128)(2,1)}, bf16[768,3072]{1,0:T(8,128)(2,1)}, bf16[1536,768]{1,0:T(8,128)(2,1)}, f32[16,768]{1,0:T(8,128)}) custom-call(s32[4]{0:T(128)} %wrows.1, s32[4]{0:T(128)} %wcols.1, bf16[14,14,768]{2,1,0:T(8,128)(2,1)} %bitcast.9, bf16[14,14,768]{2,1,0:T(8,128)(2,1)} %bitcast.10, ...), custom_call_target="tpu_custom_call" | custom-call | tf_op jit(solution)/shard_map/relay/pallas_call | solution.py:1121
  211.3 7.6 %finish.1 = (f32[768,3072]{1,0:T(8,128)}, f32[1536,768]{1,0:T(8,128)}, bf16[14,14,768]{2,1,0:T(8,128)(2,1)}, f32[14,14,1,768]{3,2,1,0:T(1,128)}, f32[9,1,768]{2,...) custom-call(bf16[768,3072]{1,0:T(8,128)(2,1)} %get-tuple-element.21.out1, ...), custom_call_target="tpu_custom_call" | custom-call | tf_op jit(solution)/shard_map/finish/pallas_call | solution.py:1257

commit v5 on v4

--- a/solution.py
+++ b/solution.py
@@ -333,7 +333,6 @@
     peers = [mate, opposite, diagonal, *nexts, *partners]
     for peer in peers:
         pl.semaphore_signal(barrier, inc=1, device_id=peer, device_id_type=MESH)
-    pl.semaphore_wait(barrier, len(peers))
 
     def remote(src, dst, send, recv, peer):
         return pltpu.make_async_remote_copy(
@@ -410,10 +409,16 @@
 
         @pl.when(c == k)
         def _():
-            local, sent = weight_copies(k)
-            for here, there in zip(local, sent):
-                here.start()
-                there.start()
+            for copy in weight_copies(k)[0]:
+                copy.start()
+
+    pl.semaphore_wait(barrier, len(peers))
+    for k in range(2):
+
+        @pl.when(c == k)
+        def _():
+            for copy in weight_copies(k)[1]:
+                copy.start()
 
     for copy in small_inputs:
         copy.wait()

time: 222 us -> 222 us (level)
  no operation moved by 1% of the time
where the time goes in v5:
time: 222 us; the launch traced here: 219 us
  Pallas kernels  218 us (98%)
    pallas_call x1, Pallas kernels, relay(): pl.pallas_call(relay_kernel, out_shape=[shape(slot, BF), shape(slot, BF),...  210 us
    pallas_call x1, Pallas kernels, finish(): pl.pallas_call(finish_kernel, out_shape=[shape(out1.shape, F32), shape(ou...  7.58 us

profile of v5, /device:TPU:0, one launch (start us, length us, event | category | flops | bytes accessed | tf_op | source)
XLA Modules:
  0.0 218.6 jit_solution(5476292887972233693)
XLA Ops:
  0.6 210.2 %relay.1 = (bf16[14,14,768]{2,1,0:T(8,128)(2,1)}, bf16[14,14,768]{2,1,0:T(8,128)(2,1)}, bf16[768,3072]{1,0:T(8,128)(2,1)}, bf16[1536,768]{1,0:T(8,128)(2,1)}, f32[16,768]{1,0:T(8,128)}) custom-call(s32[4]{0:T(128)} %wrows.1, s32[4]{0:T(128)} %wcols.1, bf16[14,14,768]{2,1,0:T(8,128)(2,1)} %bitcast.9, bf16[14,14,768]{2,1,0:T(8,128)(2,1)} %bitcast.10, ...), custom_call_target="tpu_custom_call" | custom-call | tf_op jit(solution)/shard_map/relay/pallas_call | solution.py:1126
  210.8 7.6 %finish.1 = (f32[768,3072]{1,0:T(8,128)}, f32[1536,768]{1,0:T(8,128)}, bf16[14,14,768]{2,1,0:T(8,128)(2,1)}, f32[14,14,1,768]{3,2,1,0:T(1,128)}, f32[9,1,768]{2,...) custom-call(bf16[768,3072]{1,0:T(8,128)(2,1)} %get-tuple-element.21.out1, ...), custom_call_target="tpu_custom_call" | custom-call | tf_op jit(solution)/shard_map/finish/pallas_call | solution.py:1262

commit v6 on v5

--- a/solution.py
+++ b/solution.py
@@ -590,11 +590,11 @@
     odd = c == 1
     active = (None, odd, odd, helper, None)
 
-    def where_live(sub, j, run):
+    def where_live(sub, h, j, run):
         if sub == 2:
-            pl.when(jnp.logical_not(lender) | (j >= LENT))(run)
+            pl.when(jnp.logical_not(lender) | (j >= LENT - h))(run)
         elif sub == 3:
-            pl.when(j < LENT)(run)
+            pl.when(j < LENT - h)(run)
         else:
             run()
 
@@ -692,7 +692,7 @@
                 spread(h, 0, sub, j).start()
                 deliver(h, j, sub)
 
-        where_live(sub, j, run)
+        where_live(sub, h, j, run)
 
     def event(sub, e):
         for h in range(2):
@@ -715,7 +715,7 @@
 
                     deliver(h, j, sub)
 
-                where_live(sub, j, run)
+                where_live(sub, h, j, run)
 
     def early_event(e, which):
         @pl.when(odd)
@@ -1044,8 +1044,8 @@
             for sub in subs:
 
                 def sent():
-                    where_live(sub, shard(me - sign(h) * t), lambda: scatter(h, t, sub).wait_send())
-                    where_live(sub, home(h, t), lambda: spread(h, t, sub, home(h, t)).wait_send())
+                    where_live(sub, h, shard(me - sign(h) * t), lambda: scatter(h, t, sub).wait_send())
+                    where_live(sub, h, home(h, t), lambda: spread(h, t, sub, home(h, t)).wait_send())
 
                 where_active(sub, sent)
 
@@ -1060,7 +1060,7 @@
 
             @pl.when(odd)
             def _():
-                where_live(2, j, lambda: write(h, j, 2).wait())
+                where_live(2, h, j, lambda: write(h, j, 2).wait())
 
                 @pl.when(j < half_shards)
                 def _():
@@ -1074,11 +1074,11 @@
             def _():
                 hand_over(h, j).wait_recv()
 
-            @pl.when(helper & (j < LENT))
+            @pl.when(helper & (j < LENT - h))
             def _():
                 write(h, j, 3).wait_send()
 
-            @pl.when(lender & (j < LENT))
+            @pl.when(lender & (j < LENT - h))
             def _():
                 write(h, j, 3).wait_recv()
 

time: 222 us -> 222 us (level)
  no operation moved by 1% of the time
where the time goes in v6:
time: 222 us; the launch traced here: 219 us
  Pallas kernels  218 us (98%)
    pallas_call x1, Pallas kernels, relay(): pl.pallas_call(relay_kernel, out_shape=[shape(slot, BF), shape(slot, BF),...  210 us
    pallas_call x1, Pallas kernels, finish(): pl.pallas_call(finish_kernel, out_shape=[shape(out1.shape, F32), shape(ou...  7.58 us

profile of v6, /device:TPU:0, one launch (start us, length us, event | category | flops | bytes accessed | tf_op | source)
XLA Modules:
  0.0 218.6 jit_solution(6125220358616044133)
XLA Ops:
  0.6 210.2 %relay.1 = (bf16[14,14,768]{2,1,0:T(8,128)(2,1)}, bf16[14,14,768]{2,1,0:T(8,128)(2,1)}, bf16[768,3072]{1,0:T(8,128)(2,1)}, bf16[1536,768]{1,0:T(8,128)(2,1)}, f32[16,768]{1,0:T(8,128)}) custom-call(s32[4]{0:T(128)} %wrows.1, s32[4]{0:T(128)} %wcols.1, bf16[14,14,768]{2,1,0:T(8,128)(2,1)} %bitcast.9, bf16[14,14,768]{2,1,0:T(8,128)(2,1)} %bitcast.10, ...), custom_call_target="tpu_custom_call" | custom-call | tf_op jit(solution)/shard_map/relay/pallas_call | solution.py:1126
  210.9 7.6 %finish.1 = (f32[768,3072]{1,0:T(8,128)}, f32[1536,768]{1,0:T(8,128)}, bf16[14,14,768]{2,1,0:T(8,128)(2,1)}, f32[14,14,1,768]{3,2,1,0:T(1,128)}, f32[9,1,768]{2,...) custom-call(bf16[768,3072]{1,0:T(8,128)(2,1)} %get-tuple-element.21.out1, ...), custom_call_target="tpu_custom_call" | custom-call | tf_op jit(solution)/shard_map/finish/pallas_call | solution.py:1262

commit v7 on v4

--- a/solution.py
+++ b/solution.py
@@ -712,6 +712,40 @@
 
                 where_live(sub, j, run)
 
+    def settle(sub, e):
+        for h in range(2):
+
+            @pl.when((e >= 0) & (e < n - 1))
+            def _():
+                where_live(sub, shard(me - sign(h) * e), lambda: scatter(h, e, sub).wait_send())
+
+            @pl.when((e >= n - 1) & (e < 2 * n - 1))
+            def _():
+                t = e - (n - 1)
+                j = home(h, t)
+
+                def run():
+                    @pl.when(t < n - 1)
+                    def _():
+                        spread(h, t, sub, j).wait_send()
+
+                    if sub == 1:
+
+                        @pl.when(j < half_shards)
+                        def _():
+                            hand_over(h, j).wait_send()
+
+                        @pl.when(j >= half_shards)
+                        def _():
+                            write(h, j, sub).wait()
+
+                    elif sub == 3:
+                        write(h, j, sub).wait_send()
+                    else:
+                        write(h, j, sub).wait()
+
+                where_live(sub, j, run)
+
     def early_event(e, which):
         @pl.when(odd)
         def _():
@@ -984,17 +1018,34 @@
                 copy.wait_recv()
             share(m).wait_recv()
 
+    def sent_before():
+        for k in range(2):
+
+            @pl.when(c == k)
+            def _():
+                for copy in weight_copies(k)[1]:
+                    copy.wait_send()
+                params_copy(k).wait_send()
+                for m in range(2):
+                    for _when, copy in factor_copies(1 - k, m):
+                        copy.wait_send()
+
     def ring_step(t, carry):
-        for sub in (0, 4):
-            event(sub, t + jnp.where(odd, EARLY, 0))
-        where_active(1, lambda: event(1, t + EARLY))
-        where_active(2, lambda: event(2, t + EARLY))
-        where_active(3, lambda: event(3, t))
+        for sub in (0, 4, 1, 2, 3):
+            e = t + (jnp.where(odd, EARLY, 0) if sub in (0, 4) else 0 if sub == 3 else EARLY)
+
+            def both():
+                event(sub, e)
+                settle(sub, e - 2)
+
+            where_active(sub, both)
+
         @pl.when((t >= 1) & (t < 5))
         def _():
             front_sums((t - 1) // 2, lax.rem(t - 1, 2), ubuf, msk, U, xh, sgp)
 
         pl.when(t == 5)(small_sums)
+        pl.when(t == 8)(sent_before)
 
         @pl.when((t >= 6) & (t < 8))
         def _():
@@ -1016,70 +1067,27 @@
 
         return carry
 
-    lax.fori_loop(0, 2 * n - 1, ring_step, 0)
+    lax.fori_loop(0, 2 * n + 1, ring_step, 0)
     outs[...] = acc[rounds]
-
-    for k in range(2):
-
-        @pl.when(c == k)
-        def _():
-            for copy in weight_copies(k)[1]:
-                copy.wait_send()
-            params_copy(k).wait_send()
-            for m in range(2):
-                for _when, copy in factor_copies(1 - k, m):
-                    copy.wait_send()
-
     give.wait_send()
     for r in range(rounds):
         small(r).wait_send()
 
-    def drain(t, carry):
+
+    def received(j, carry):
         for h in range(2):
-            for sub in subs:
-
-                def sent():
-                    where_live(sub, shard(me - sign(h) * t), lambda: scatter(h, t, sub).wait_send())
-                    where_live(sub, home(h, t), lambda: spread(h, t, sub, home(h, t)).wait_send())
-
-                where_active(sub, sent)
+
+            @pl.when(jnp.logical_not(odd) & (j < half_shards))
+            def _():
+                hand_over(h, j).wait_recv()
+
+            @pl.when(lender & (j < LENT))
+            def _():
+                write(h, j, 3).wait_recv()
 
         return carry
 
-    lax.fori_loop(0, n - 1, drain, 0)
-
-    def written(j, carry):
-        for h in range(2):
-            write(h, j, 0).wait()
-            write(h, j, 4).wait()
-
-            @pl.when(odd)
-            def _():
-                where_live(2, j, lambda: write(h, j, 2).wait())
-
-                @pl.when(j < half_shards)
-                def _():
-                    hand_over(h, j).wait_send()
-
-                @pl.when(j >= half_shards)
-                def _():
-                    write(h, j, 1).wait()
-
-            @pl.when(jnp.logical_not(odd) & (j < half_shards))
-            def _():
-                hand_over(h, j).wait_recv()
-
-            @pl.when(helper & (j < LENT))
-            def _():
-                write(h, j, 3).wait_send()
-
-            @pl.when(lender & (j < LENT))
-            def _():
-                write(h, j, 3).wait_recv()
-
-        return carry
-
-    lax.fori_loop(0, n, written, 0)
+    lax.fori_loop(0, n, received, 0)
 
     @pl.when(lender)
     def _():

time: 222 us -> 222 us (level)
  no operation moved by 1% of the time
where the time goes in v7:
time: 222 us; the launch traced here: 219 us
  Pallas kernels  218 us (98%)
    pallas_call x1, Pallas kernels, relay(): pl.pallas_call(relay_kernel, out_shape=[shape(slot, BF), shape(slot, BF),...  211 us
    pallas_call x1, Pallas kernels, finish(): pl.pallas_call(finish_kernel, out_shape=[shape(out1.shape, F32), shape(ou...  7.58 us

profile of v7, /device:TPU:0, one launch (start us, length us, event | category | flops | bytes accessed | tf_op | source)
XLA Modules:
  0.0 218.9 jit_solution(9718932058541176576)
XLA Ops:
  0.6 210.5 %relay.1 = (bf16[14,14,768]{2,1,0:T(8,128)(2,1)}, bf16[14,14,768]{2,1,0:T(8,128)(2,1)}, bf16[768,3072]{1,0:T(8,128)(2,1)}, bf16[1536,768]{1,0:T(8,128)(2,1)}, f32[16,768]{1,0:T(8,128)}) custom-call(s32[4]{0:T(128)} %wrows.1, s32[4]{0:T(128)} %wcols.1, bf16[14,14,768]{2,1,0:T(8,128)(2,1)} %bitcast.9, bf16[14,14,768]{2,1,0:T(8,128)(2,1)} %bitcast.10, ...), custom_call_target="tpu_custom_call" | custom-call | tf_op jit(solution)/shard_map/relay/pallas_call | solution.py:1129
  211.2 7.6 %finish.1 = (f32[768,3072]{1,0:T(8,128)}, f32[1536,768]{1,0:T(8,128)}, bf16[14,14,768]{2,1,0:T(8,128)(2,1)}, f32[14,14,1,768]{3,2,1,0:T(1,128)}, f32[9,1,768]{2,...) custom-call(bf16[768,3072]{1,0:T(8,128)(2,1)} %get-tuple-element.21.out1, ...), custom_call_target="tpu_custom_call" | custom-call | tf_op jit(solution)/shard_map/finish/pallas_call | solution.py:1265

commit v8 on v6

--- a/solution.py
+++ b/solution.py
@@ -741,14 +741,13 @@
             if t == FF // FTILE * 2 // 3 - 1 and order == range(FF // FTILE):
                 start_factors(m, "X0")
         wait(last)
-        for i in range(2):
-            cols = pl.ds(i * D // 2, D // 2)
-            part = total[:, i * D // 2 : (i + 1) * D // 2]
-            gout[jnp.where(early, m, 2 + m), :, cols] = (part + dot(before, w2[pl.ds(last * FTILE, FTILE), cols])).astype(BF)
-
-            @pl.when(early)
-            def _():
-                u_hop(m)[i].start()
+        total = total + dot(before, w2[pl.ds(last * FTILE, FTILE), :])
+        gout[jnp.where(early, m, 2 + m)] = total.astype(BF)
+
+        @pl.when(early)
+        def _():
+            for copy in u_hop(m):
+                copy.start()
 
     def give_results(m):
         @pl.when(early)
@@ -1258,7 +1257,7 @@
     anywhere = pl.BlockSpec(memory_space=pl.ANY)
     line = (1, D)
     spread = slot[:2] + line
-    steps = 16
+    steps = 8
     return pl.pallas_call(
         finish_kernel,
         out_shape=[

time: 222 us -> 222 us (level)
  no operation moved by 1% of the time
where the time goes in v8:
time: 222 us; the launch traced here: 218 us
  Pallas kernels  217 us (98%)
    pallas_call x1, Pallas kernels, relay(): pl.pallas_call(relay_kernel, out_shape=[shape(slot, BF), shape(slot, BF),...  210 us
    pallas_call x1, Pallas kernels, finish(): pl.pallas_call(finish_kernel, out_shape=[shape(out1.shape, F32), shape(ou...  7.4 us

profile of v8, /device:TPU:0, one launch (start us, length us, event | category | flops | bytes accessed | tf_op | source)
XLA Modules:
  0.0 218.1 jit_solution(8875213191217338512)
XLA Ops:
  0.6 209.9 %relay.1 = (bf16[14,14,768]{2,1,0:T(8,128)(2,1)}, bf16[14,14,768]{2,1,0:T(8,128)(2,1)}, bf16[768,3072]{1,0:T(8,128)(2,1)}, bf16[1536,768]{1,0:T(8,128)(2,1)}, f32[16,768]{1,0:T(8,128)}) custom-call(s32[4]{0:T(128)} %wrows.1, s32[4]{0:T(128)} %wcols.1, bf16[14,14,768]{2,1,0:T(8,128)(2,1)} %bitcast.9, bf16[14,14,768]{2,1,0:T(8,128)(2,1)} %bitcast.10, ...), custom_call_target="tpu_custom_call" | custom-call | tf_op jit(solution)/shard_map/relay/pallas_call | solution.py:1125
  210.5 7.4 %finish.1 = (f32[768,3072]{1,0:T(8,128)}, f32[1536,768]{1,0:T(8,128)}, bf16[14,14,768]{2,1,0:T(8,128)(2,1)}, f32[14,14,1,768]{3,2,1,0:T(1,128)}, f32[9,1,768]{2,...) custom-call(bf16[768,3072]{1,0:T(8,128)(2,1)} %get-tuple-element.21.out1, ...), custom_call_target="tpu_custom_call" | custom-call | tf_op jit(solution)/shard_map/finish/pallas_call | solution.py:1261
